TPU v7x, 128 devices: a whole 4x4x4 slice. The times are simulated.
128 devices in a mesh: gx: 8 (over z_lo, x), gy: 16 (over z_hi, y, core).
Axes of the slice: x: 4, y: 4, z: 4 (z_hi: 2, z_lo: 2; z = z_hi * 2 + z_lo), core: 2. Of those that a mesh axis runs over, the one named last changes fastest.
Arguments:
- initial_state: float32 [4, 4, 32, 128, 1024], P(None, None, None, 'gy', 'gx'), may hold values from -6 to 6
- forcing: float32 [4, 4, 32, 128, 1024], P(None, None, None, 'gy', 'gx'), may hold values from -6 to 6
- jacobian: float32 [4, 4, 128, 1024], P(None, None, 'gy', 'gx'), may hold values from 0.5 to 2
- metric: float32 [4, 4, 128, 1024], P(None, None, 'gy', 'gx'), may hold values from 0.5 to 2
- viscosity: float32 [32], replicated, may hold values from 0.0001 to 0.0006
- element_turns: int32 [128, 1024], P('gy', 'gx'), may hold values from 0 to 3
Outputs:
- final_state: float32 [4, 4, 32, 128, 1024], P(None, None, None, 'gy', 'gx')
Inputs may be any that keep to these rules, and one draw needn't show every extreme that they name: `element_turns`: quarter turns from an element's stored node order to its face's node order.
All inputs are finite; a program needn't handle non-finite values.
Results may differ from a plain program's by a relative error of at most 0.0001.
Values sent between devices are 32-bit elements; how exact they have to be, the bound alone decides.
A program may use at most 128 MiB of HBM per device.

v0:
```python
import functools
import math

import jax
import jax.numpy as jnp
import numpy as np
from jax import lax
from jax.experimental import pallas as pl
from jax.experimental.pallas import tpu as pltpu
from jax.sharding import PartitionSpec as P

NP = 4
SECTIONS = 5
GROUPS = 4
UNROLL = 8
time_step = 1.0
PAIRS = ((0, 1), (0, 2), (0, 3), (1, 2), (1, 3), (2, 3))
NORTH, SOUTH, EAST, WEST, NE, SW, NW, SE = range(8)
STEP = ((0, 1), (0, -1), (1, 0), (-1, 0), (1, 1), (-1, -1), (-1, 1), (1, -1))
MESH = pl.DeviceIdType.MESH
RIGHT = (EAST, NE, SE)


def lagrange_tables():
    root_five = 1.0 / math.sqrt(5.0)
    points = np.array([-1.0, -root_five, root_five, 1.0])
    weights = np.array([1.0 / 6.0, 5.0 / 6.0, 5.0 / 6.0, 1.0 / 6.0])
    number = points.shape[0]
    products = np.ones(number)
    for row in range(number):
        for other in range(number):
            if other != row:
                products[row] = products[row] * (points[row] - points[other])
    derivative = np.zeros((number, number))
    for row in range(number):
        for column in range(number):
            if row == column:
                derivative[row, column] = sum(
                    1.0 / (points[row] - points[other])
                    for other in range(number)
                    if other != row
                )
            else:
                derivative[row, column] = products[row] / (
                    products[column] * (points[row] - points[column])
                )
    return (derivative, weights)


def turned(v):
    return [[v[i][NP - 1 - j] for i in range(NP)] for j in range(NP)]


def face_frame(v, masks):
    result = v
    for mask in masks:
        v = turned(v)
        result = [
            [jnp.where(mask, v[j][i], result[j][i]) for i in range(NP)]
            for j in range(NP)
        ]
    return result


def kernel(
    sizes,
    state_hbm,
    forcing_hbm,
    jacobian_hbm,
    metric_hbm,
    turns_hbm,
    viscosity_hbm,
    out_ref,
    state_ref,
    forcing_ref,
    jacobian_ref,
    metric_ref,
    turns_ref,
    viscosity_ref,
    field_sem,
    small_sem,
    part_ref,
    base_ref,
    tend_ref,
    inverse_ref,
    own_k_ref,
    both_k_ref,
    diagonal_ref,
    mass_ref,
    out_rows,
    out_tiles,
    in_rows,
    in_tiles,
    send_sem,
    recv_sem,
    set_out_rows,
    set_out_tiles,
    set_in_rows,
    set_in_tiles,
    set_send,
    set_recv,
    ini_out_rows,
    ini_out_tiles,
    ini_in_rows,
    ini_in_tiles,
    ini_send,
    ini_recv,
):
    chan, rows, cols, count_x, count_y = sizes
    per = chan // GROUPS
    last_row, last_col = rows - 1, cols - 1
    derivative, weights = lagrange_tables()
    cx = lax.axis_index("gx")
    cy = lax.axis_index("gy")
    lane = lax.broadcasted_iota(jnp.int32, (rows, cols), 1)
    sub = lax.broadcasted_iota(jnp.int32, (rows, cols), 0)
    at_west, at_east = lane == 0, lane == last_col
    at_south, at_north = sub == 0, sub == last_row
    zero = jnp.zeros((rows, cols), jnp.float32)
    there_north = cy < count_y - 1
    there_south = cy > 0

    def device(d):
        dx, dy = STEP[d]
        return (lax.rem(cx + dx + count_x, count_x), cy + dy)

    def for_each(todo):
        for d in (EAST, WEST):
            todo(d)

        @pl.when(there_north)
        def _():
            for d in (NORTH, NE, NW):
                todo(d)

        @pl.when(there_south)
        def _():
            for d in (SOUTH, SE, SW):
                todo(d)

    def copy(bufs, where_out, where_in, d, arriving=False):
        o_rows, o_tiles, i_rows, i_tiles, ssem, rsem, shared = bufs
        slot = d if arriving else d ^ 1
        if d in (NORTH, SOUTH):
            src, dst = o_rows.at[(d,) + where_out], i_rows.at[(slot,) + where_in]
        else:
            src = o_tiles.at[(d - 2 if shared is None else int(d not in RIGHT),) + where_out]
            dst = i_tiles.at[(slot - 2,) + where_in]
        return pltpu.make_async_remote_copy(
            src_ref=src,
            dst_ref=dst,
            send_sem=ssem.at[(d,) + where_out],
            recv_sem=rsem.at[(slot,) + where_in],
            device_id=device(d),
            device_id_type=MESH,
        )

    def start(bufs, where_out, where_in):
        for_each(lambda d: copy(bufs, where_out, where_in, d).start())

    def finish(bufs, where_out, where_in):
        def todo(d):
            c = copy(bufs, where_out, where_in, d, arriving=True)
            c.wait_recv()
            c.wait_send()

        for_each(todo)

    main = (out_rows, out_tiles, in_rows, in_tiles, send_sem, recv_sem, True)
    sets = (set_out_rows, set_out_tiles, set_in_rows, set_in_tiles, set_send, set_recv, True)
    ini = (ini_out_rows, ini_out_tiles, ini_in_rows, ini_in_tiles, ini_send, ini_recv, None)

    def join_x(a, b):
        return (
            a + jnp.where(at_west, 0.0, pltpu.roll(b, 1, 1)),
            b + jnp.where(at_east, 0.0, pltpu.roll(a, cols - 1, 1)),
        )

    def join_y(a, b):
        return (
            a + jnp.where(at_south, 0.0, pltpu.roll(b, 1, 0)),
            b + jnp.where(at_north, 0.0, pltpu.roll(a, rows - 1, 0)),
        )

    def join(s):
        s = [list(r) for r in s]
        for j in range(NP):
            s[j][0], s[j][3] = join_x(s[j][0], s[j][3])
        for i in range(NP):
            s[0][i], s[3][i] = join_y(s[0][i], s[3][i])
        return s

    def line(v, k):
        p = [k[n] * (v[b] - v[a]) for n, (a, b) in enumerate(PAIRS)]
        return (
            p[0] + p[1] + p[2],
            p[3] + p[4] - p[0],
            p[5] - p[1] - p[3],
            -(p[2] + p[4] + p[5]),
        )

    def stiff(v, k_ref):
        s = [[None] * NP for _ in range(NP)]
        for j in range(NP):
            got = line(v[j], [k_ref[j * 6 + n] for n in range(6)])
            for i in range(NP):
                s[j][i] = got[i]
        for i in range(NP):
            got = line(
                [v[j][i] for j in range(NP)],
                [k_ref[24 + i * 6 + n] for n in range(6)],
            )
            for j in range(NP):
                s[j][i] = s[j][i] + got[j]
        return join(s)

    def from_inside(w):
        rx = [[None] * NP for _ in range(NP)]
        ry = [[None] * NP for _ in range(NP)]
        for j in range(NP):
            k = [both_k_ref[j * 6 + n] for n in range(6)]
            rx[j][0] = k[0] * w[j][1] + k[1] * w[j][2] + k[2] * w[j][3]
            rx[j][3] = k[2] * w[j][0] + k[4] * w[j][1] + k[5] * w[j][2]
        for i in range(NP):
            k = [both_k_ref[24 + i * 6 + n] for n in range(6)]
            ry[0][i] = k[0] * w[1][i] + k[1] * w[2][i] + k[2] * w[3][i]
            ry[3][i] = k[2] * w[0][i] + k[4] * w[1][i] + k[5] * w[2][i]
        return joined_edges(rx, ry)

    def joined_edges(rx, ry):
        for i in (0, 3):
            rx[0][i], rx[3][i] = join_y(rx[0][i], rx[3][i])
        for j in (0, 3):
            ry[j][0], ry[j][3] = join_x(ry[j][0], ry[j][3])
        return rx, ry

    def load(ref, c):
        return [[ref[j, i, c] for i in range(NP)] for j in range(NP)]

    def store(ref, c, v):
        for j in range(NP):
            for i in range(NP):
                ref[j, i, c] = v[j][i]

    def times(v, ref):
        return [[v[j][i] * ref[j * NP + i] for i in range(NP)] for j in range(NP)]

    def lay_rows(ref, where, k, top, bottom):
        ref[(NORTH,) + where + (slice(k, k + 1), slice(None))] = top[last_row:, :]
        ref[(SOUTH,) + where + (slice(k, k + 1), slice(None))] = bottom[0:1, :]

    def lay_lane(tiles, n, right, left, corner):
        here = lane == n
        from_right = lax.rem(n + 1, cols)

        def put(d, v, shift):
            tiles[d - 2] = jnp.where(here, pltpu.roll(v, shift, 1), tiles[d - 2])

        if right is not None:
            put(EAST, right, from_right)
            put(WEST, left, n)
        if corner is not None:
            put(NE, corner[0], from_right)
            put(SW, corner[1], n)
            put(NW, corner[2], n)
            put(SE, corner[3], from_right)

    def emit(refs, where, c, tiles, fields):
        for q, (vx, vy, corner) in enumerate(fields):
            for i in range(NP):
                lay_rows(refs[0], where + (c,), q * NP + i, vy[3][i], vy[0][i])
        sides = []
        for tile, i in zip(tiles, (3, 0)):
            (v, _, _), (x, _, corner) = fields
            top, bottom = (corner[0], corner[3]) if i == 3 else (corner[2], corner[1])
            ends = jnp.where(
                sub == last_row,
                v[3][i],
                jnp.where(
                    sub == last_row - 1,
                    pltpu.roll(x[3][i], rows - 1, 0),
                    jnp.where(sub == last_row - 2, pltpu.roll(top, rows - 2, 0), bottom),
                ),
            )
            for m, value in enumerate([f[0][j][i] for f in fields for j in range(3)] + [ends]):
                n = m * per + c
                shift = lax.rem(n + 1, cols) if i == 3 else n
                tile = jnp.where(lane == n, pltpu.roll(value, shift, 1), tile)
            sides.append(tile)
        return tuple(sides)

    def corners_of(v):
        return (v[3][3], v[0][0], v[3][0], v[0][3])

    def row(ref, where, k):
        return jnp.broadcast_to(
            ref[where + (slice(k, k + 1), slice(None))], (rows, cols)
        )

    def ini_tiles():
        got = [ini_in_tiles[d - 2] for d in range(2, 8)]
        for d in (NE, NW):
            got[d - 2] = pltpu.roll(got[d - 2], rows - 1, 0)
        for d in (SE, SW):
            got[d - 2] = pltpu.roll(got[d - 2], 1, 0)
        return got

    def in_sides(ref, where):
        sides = []
        for side, above, below in ((EAST, NE, SE), (WEST, NW, SW)):
            here, up, down = [ref[(d - 2,) + where] for d in (side, above, below)]
            first = pltpu.roll(pltpu.roll(up, 6 * per, 1), rows - 1, 0)
            ends = jnp.where(
                sub == last_row,
                here + first,
                jnp.where(
                    sub == last_row - 1,
                    here + pltpu.roll(up, rows - 2, 0),
                    jnp.where(sub == 0, pltpu.roll(down, 1, 0), pltpu.roll(down, 4, 0)),
                ),
            )
            sides.append(jnp.where(lane < 6 * per, here, ends))
        return sides

    def add_in(v, ref, where, c, got, q):
        v = [list(r) for r in v]
        for i in range(NP):
            k = q * NP + i
            v[3][i] = v[3][i] + jnp.where(at_north, row(ref, (NORTH,) + where + (c,), k), 0.0)
            v[0][i] = v[0][i] + jnp.where(at_south, row(ref, (SOUTH,) + where + (c,), k), 0.0)
        for side, i, to, edge in ((0, 3, last_col, at_east), (1, 0, cols, at_west)):

            def lane_to(m):
                return pltpu.roll(got[side], lax.rem(to - (m * per + c), cols), 1)

            column = [lane_to(q * 3 + j) for j in range(3)]
            ends = lane_to(6)
            if q == 1:
                top, bottom = pltpu.roll(ends, 1, 0), pltpu.roll(ends, rows - 1, 0)
            else:
                top = bottom = ends
            for j in (1, 2):
                v[j][i] = v[j][i] + jnp.where(edge, column[j], 0.0)
            v[0][i] = v[0][i] + jnp.where(
                edge, jnp.where(at_south, column[0] + bottom, column[0]), 0.0
            )
            v[3][i] = v[3][i] + jnp.where(
                edge, jnp.where(at_north, top, pltpu.roll(column[0], rows - 1, 0)), 0.0
            )
        return v

    def keep_tiles(ref, where, tiles):
        for side in range(2):
            ref[(side,) + where] = tiles[side]

    small = [
        pltpu.make_async_copy(a, b, small_sem.at[n])
        for n, (a, b) in enumerate(
            (
                (jacobian_hbm, jacobian_ref),
                (metric_hbm, metric_ref),
                (turns_hbm, turns_ref),
                (viscosity_hbm, viscosity_ref),
            )
        )
    ]
    for c in small:
        c.start()

    def fields(g):
        part = (slice(None), slice(None), pl.ds(g * per, per))
        return [
            pltpu.make_async_copy(a.at[part], b.at[part], field_sem.at[n, g])
            for n, (a, b) in enumerate(
                ((state_hbm, state_ref), (forcing_hbm, forcing_ref))
            )
        ]

    for g in range(GROUPS):
        for c in fields(g):
            c.start()

    in_rows[...] = jnp.zeros_like(in_rows)
    in_tiles[...] = jnp.zeros_like(in_tiles)
    set_in_rows[...] = jnp.zeros_like(set_in_rows)
    set_in_tiles[...] = jnp.zeros_like(set_in_tiles)
    ini_in_rows[...] = jnp.zeros_like(ini_in_rows)
    ini_in_tiles[...] = jnp.zeros_like(ini_in_tiles)
    barrier = pltpu.get_barrier_semaphore()
    for_each(
        lambda d: pl.semaphore_signal(
            barrier, inc=1, device_id=device(d), device_id_type=MESH
        )
    )
    for c in small:
        c.wait()

    turns = turns_ref[...]
    masks = [turns == quarter for quarter in range(1, 4)]
    jacobian = face_frame(
        [[jacobian_ref[j, i] for i in range(NP)] for j in range(NP)], masks
    )
    metric = face_frame(
        [[metric_ref[j, i] for i in range(NP)] for j in range(NP)], masks
    )
    mass = [
        [float(weights[j] * weights[i]) * jacobian[j][i] for i in range(NP)]
        for j in range(NP)
    ]
    flux = [
        [float(weights[j] * weights[i]) * metric[j][i] for i in range(NP)]
        for j in range(NP)
    ]
    for j in range(NP):
        for i in range(NP):
            mass_ref[j * NP + i] = mass[j][i]

    def coefficients(f):
        return [
            sum(float(-derivative[n, a] * derivative[n, b]) * f[n] for n in range(NP))
            for a, b in PAIRS
        ]

    kx = [coefficients(flux[j]) for j in range(NP)]
    ky = [coefficients([flux[j][i] for j in range(NP)]) for i in range(NP)]
    for m in range(NP):
        for n in range(6):
            own_k_ref[m * 6 + n] = kx[m][n]
            own_k_ref[24 + m * 6 + n] = ky[m][n]
    first = lambda k: k[0] + k[1] + k[2]
    final = lambda k: k[2] + k[4] + k[5]
    dx = [[first(kx[j]), None, None, final(kx[j])] for j in range(NP)]
    dy = [[None] * NP for _ in range(NP)]
    for i in range(NP):
        dy[0][i], dy[3][i] = first(ky[i]), final(ky[i])
    dx, dy = joined_edges(dx, dy)
    local = join(mass)
    tiles = [zero] * 6
    for n in range(NP):
        lay_rows(ini_out_rows, (0,), n, local[3][n], local[0][n])
        lay_rows(ini_out_rows, (0,), 4 + n, dy[3][n], dy[0][n])
        lay_lane(tiles, n, local[n][3], local[n][0], None)
        lay_lane(tiles, 4 + n, dx[n][3], dx[n][0], None)
    for n in range(6):
        lay_rows(ini_out_rows, (1,), n, kx[3][n], kx[0][n])
        lay_lane(tiles, 8 + n, ky[3][n], ky[0][n], None)
    lay_lane(tiles, 0, None, None, corners_of(local))
    both = [[None] * NP for _ in range(NP)]
    for j in (0, 3):
        for i in (0, 3):
            both[j][i] = dx[j][i] + dy[j][i]
    lay_lane(tiles, 1, None, None, corners_of(both))
    for n in (6, 7):
        lay_rows(ini_out_rows, (1,), n, zero, zero)
    for d in range(2, 8):
        ini_out_tiles[d - 2] = tiles[d - 2]
    peers = 2 + 3 * there_north.astype(jnp.int32) + 3 * there_south.astype(jnp.int32)
    pl.semaphore_wait(barrier, peers)
    start(ini, (), ())

    def enter_group(g):
        for c in fields(g):
            c.wait()

        def enter(c, tiles):
            ch = g * per + c
            state = face_frame(load(state_ref, ch), masks)
            forcing = face_frame(load(forcing_ref, ch), masks)
            base = join(times(state, mass_ref))
            tend = join(times(forcing, mass_ref))
            store(base_ref, ch, base)
            store(tend_ref, ch, tend)
            tiles = emit(
                sets,
                (g,),
                c,
                tiles,
                ((base, base, corners_of(base)), (tend, tend, corners_of(tend))),
            )
            store(part_ref, ch, stiff(state, own_k_ref))
            return tiles

        tiles = lax.fori_loop(0, per, enter, (zero,) * 2, unroll=UNROLL)
        keep_tiles(set_out_tiles, (g,), tiles)
        start(sets, (g,), (g,))

    pl.loop(0, GROUPS)(enter_group)

    finish(ini, (), ())
    got = ini_tiles()

    def lane_of(d, n):
        to = last_col if d in (EAST, NE, SE) else 0
        return pltpu.roll(got[d - 2], (to - n) % cols, 1)

    def north(block, k):
        return jnp.where(at_north, row(ini_in_rows, (NORTH, block), k), 0.0)

    def south(block, k):
        return jnp.where(at_south, row(ini_in_rows, (SOUTH, block), k), 0.0)

    def east(n):
        return jnp.where(at_east, lane_of(EAST, n), 0.0)

    def west(n):
        return jnp.where(at_west, lane_of(WEST, n), 0.0)

    def with_neighbours(v, first_k, corner_n):
        v = [list(r) for r in v]
        for i in range(NP):
            v[3][i] = v[3][i] + north(0, first_k + i)
            v[0][i] = v[0][i] + south(0, first_k + i)
        for j in range(NP):
            v[j][3] = v[j][3] + east(first_k + j)
            v[j][0] = v[j][0] + west(first_k + j)
        for d, j, i, m in (
            (NE, 3, 3, at_north & at_east),
            (SW, 0, 0, at_south & at_west),
            (NW, 3, 0, at_north & at_west),
            (SE, 0, 3, at_south & at_east),
        ):
            v[j][i] = v[j][i] + jnp.where(m, lane_of(d, corner_n), 0.0)
        return v

    assembled = with_neighbours(local, 0, 0)
    diagonal = with_neighbours([[zero] * NP for _ in range(NP)], 4, 1)
    for j in range(NP):
        for i in range(NP):
            inverse_ref[j * NP + i] = 1.0 / assembled[j][i]
            diagonal_ref[j * NP + i] = diagonal[j][i]
    for m in range(NP):
        for n in range(6):
            x, y = kx[m][n], ky[m][n]
            if m == 0:
                x, y = x + south(1, n), y + west(8 + n)
            if m == 3:
                x, y = x + north(1, n), y + east(8 + n)
            both_k_ref[m * 6 + n] = x
            both_k_ref[24 + m * 6 + n] = y

    def emit_main(g, c, tiles, s):
        rx, ry = from_inside(times(s, inverse_ref))
        corner = tuple(
            rx[j][i] + ry[j][i] for j, i in ((3, 3), (0, 0), (3, 0), (0, 3))
        )
        return emit(main, (g,), c, tiles, ((s, s, corners_of(s)), (rx, ry, corner)))

    def send_group(g):
        def send(c, tiles):
            return emit_main(g, c, tiles, load(part_ref, g * per + c))

        tiles = lax.fori_loop(0, per, send, (zero,) * 2, unroll=UNROLL)
        keep_tiles(out_tiles, (g,), tiles)
        start(main, (g,), (0, g))

    pl.loop(0, GROUPS)(send_group)

    def settle_group(g):
        finish(sets, (g,), (g,))
        got = in_sides(set_in_tiles, (g,))

        def settle(c, carry):
            ch = g * per + c
            for q, ref in enumerate((base_ref, tend_ref)):
                v = add_in(load(ref, ch), set_in_rows, (g,), c, got, q)
                store(ref, ch, times(v, inverse_ref))
            return carry

        lax.fori_loop(0, per, settle, 0, unroll=UNROLL)

    pl.loop(0, GROUPS)(settle_group)

    def advance(ch, c, g, parity, got, factor):
        where = (parity, g)
        s = add_in(load(part_ref, ch), in_rows, where, c, got, 0)
        w = times(s, inverse_ref)
        t = add_in(stiff(w, both_k_ref), in_rows, where, c, got, 1)
        scale = factor * viscosity_ref[ch]
        for j in range(NP):
            for i in range(NP):
                if j in (0, 3) or i in (0, 3):
                    t[j][i] = t[j][i] - diagonal_ref[j * NP + i] * w[j][i]
        return [
            [
                base_ref[j, i, ch]
                + (
                    factor * tend_ref[j, i, ch]
                    - scale * (t[j][i] * inverse_ref[j * NP + i])
                )
                for i in range(NP)
            ]
            for j in range(NP)
        ]

    def section_group(step):
        section, g = step // GROUPS, lax.rem(step, GROUPS)
        parity = lax.rem(section, 2)
        factor = jnp.float32(time_step / SECTIONS)
        for m in range(1, SECTIONS - 1):
            factor = jnp.where(
                section == m, jnp.float32(time_step / (SECTIONS - m)), factor
            )
        finish(main, (g,), (parity, g))
        got = in_sides(in_tiles, (parity, g))

        def body(c, tiles):
            ch = g * per + c
            u = advance(ch, c, g, parity, got, factor)
            s = stiff(u, own_k_ref)
            store(part_ref, ch, s)
            return emit_main(g, c, tiles, s)

        tiles = lax.fori_loop(0, per, body, (zero,) * 2, unroll=UNROLL)
        keep_tiles(out_tiles, (g,), tiles)
        start(main, (g,), (1 - parity, g))

    pl.loop(0, (SECTIONS - 1) * GROUPS)(section_group)

    def last_group(g):
        parity = (SECTIONS - 1) % 2
        finish(main, (g,), (parity, g))
        got = in_sides(in_tiles, (parity, g))

        def body(c, carry):
            ch = g * per + c
            store(out_ref, ch, advance(ch, c, g, parity, got, jnp.float32(time_step)))
            return carry

        lax.fori_loop(0, per, body, 0, unroll=UNROLL)

    pl.loop(0, GROUPS)(last_group)


def on_device(
    counts, initial_state, forcing, jacobian, metric, viscosity, element_turns
):
    np0, np1, chan, rows, cols = initial_state.shape
    per = chan // GROUPS
    f32 = jnp.float32
    field = pltpu.VMEM((NP, NP, chan, rows, cols), f32)
    vmem = pl.BlockSpec(memory_space=pltpu.VMEM)

    def buffers(out_lead, in_lead, tiles_per_rows, out_tiles):
        dma = pltpu.SemaphoreType.DMA
        return [
            pltpu.VMEM((2,) + out_lead + (tiles_per_rows, rows, cols), f32),
            pltpu.VMEM((out_tiles,) + out_lead + (rows, cols), f32),
            pltpu.VMEM((2,) + in_lead + (tiles_per_rows, rows, cols), f32),
            pltpu.VMEM((6,) + in_lead + (rows, cols), f32),
            dma((8,) + out_lead),
            dma((8,) + in_lead),
        ]

    return pl.pallas_call(
        functools.partial(kernel, (chan, rows, cols) + counts),
        out_shape=jax.ShapeDtypeStruct(initial_state.shape, f32),
        in_specs=[pl.BlockSpec(memory_space=pl.ANY)] * 6,
        out_specs=vmem,
        scratch_shapes=[
            field,
            field,
            pltpu.VMEM(jacobian.shape, f32),
            pltpu.VMEM(metric.shape, f32),
            pltpu.VMEM(element_turns.shape, jnp.int32),
            pltpu.SMEM(viscosity.shape, f32),
            pltpu.SemaphoreType.DMA((2, GROUPS)),
            pltpu.SemaphoreType.DMA((4,)),
            field,
            field,
            field,
            pltpu.VMEM((16, rows, cols), f32),
            pltpu.VMEM((48, rows, cols), f32),
            pltpu.VMEM((48, rows, cols), f32),
            pltpu.VMEM((16, rows, cols), f32),
            pltpu.VMEM((16, rows, cols), f32),
        ]
        + buffers((GROUPS,), (2, GROUPS), per, 2)
        + buffers((GROUPS,), (GROUPS,), per, 2)
        + buffers((), (), 2, 6),
        compiler_params=pltpu.CompilerParams(
            collective_id=0, has_side_effects=True, vmem_limit_bytes=56 * 2**20
        ),
    )(initial_state, forcing, jacobian, metric, element_turns, viscosity)


def solution(mesh):
    placed = (
        P(None, None, None, "gy", "gx"),
        P(None, None, None, "gy", "gx"),
        P(None, None, "gy", "gx"),
        P(None, None, "gy", "gx"),
        P(),
        P("gy", "gx"),
    )
    return jax.shard_map(
        functools.partial(on_device, (mesh.shape["gx"], mesh.shape["gy"])),
        mesh=mesh,
        in_specs=placed,
        out_specs=P(None, None, None, "gy", "gx"),
        check_vma=False,
    )
```

profile of v0, /device:TPU:25, one launch (start us, length us, event | category | flops | bytes accessed | tf_op | source)
XLA Modules:
  0.0 51.8 jit_solution(12807816572150187551)
XLA Ops:
  0.0 48.7 %shard_map.64 = f32[4,4,32,8,128]{4,3,2,1,0:T(8,128)} custom-call(f32[4,4,32,8,128]{4,3,2,1,0:T(8,128)} %state_hbm.1, f32[4,4,32,8,128]{4,3,2,1,0:T(8,128)} %forcing_hbm.1, f32[4,4,8,128]{3,2,1,0:T(8,128)} %jacobian_hbm.1, f32[4,4,8,128]{3,2,1,0:T(8,128)} %metric_hbm.1, s32[8,128]{1,0:T(8,128)} %turns_hbm.1, f32[32]{0:T(128)} %viscosity_hbm.1), custom_call_target="tpu_custom_call" | custom-call | tf_op jit(solution)/shard_map/pallas_call | solution.py:654
  48.7 3.1 %copy.8 = f32[4,4,32,8,128]{4,3,2,1,0:T(8,128)} copy(f32[4,4,32,8,128]{4,3,2,1,0:T(8,128)} %shard_map.64) | data formatting | bytes 4194304
where the time goes:
time: 52 us; the launch traced here: 51.8 us
  Pallas kernels  48.7 us (94%)
  local copies, waits for them, and re-layouts  3.11 us (6%)
    pallas_call x1, Pallas kernels, on_device(): pl.pallas_call(functools.partial(kernel, (chan, rows, cols) + counts), ou...  48.7 us
    unnamed x1, local copies, waits for them, and re-layouts  3.11 us

commit v1 on v0

--- a/solution.py
+++ b/solution.py
@@ -19,6 +19,7 @@
 STEP = ((0, 1), (0, -1), (1, 0), (-1, 0), (1, 1), (-1, -1), (-1, 1), (1, -1))
 MESH = pl.DeviceIdType.MESH
 RIGHT = (EAST, NE, SE)
+TILES_N, TILES_S = 8, 9
 
 
 def lagrange_tables():
@@ -87,10 +88,12 @@
     both_k_ref,
     diagonal_ref,
     mass_ref,
+    weight_ref,
     out_rows,
     out_tiles,
     in_rows,
     in_tiles,
+    in_more,
     send_sem,
     recv_sem,
     set_out_rows,
@@ -103,6 +106,7 @@
     ini_out_tiles,
     ini_in_rows,
     ini_in_tiles,
+    ini_in_more,
     ini_send,
     ini_recv,
 ):
@@ -121,54 +125,73 @@
     there_south = cy > 0
 
     def device(d):
-        dx, dy = STEP[d]
+        dx, dy = STEP[d % 8]
         return (lax.rem(cx + dx + count_x, count_x), cy + dy)
 
-    def for_each(todo):
+    def for_each(todo, tiles_too=False):
+        @pl.when(there_north)
+        def _():
+            for d in (NE, NW, NORTH) + (TILES_N,) * tiles_too:
+                todo(d)
+
+        @pl.when(there_south)
+        def _():
+            for d in (SE, SW, SOUTH) + (TILES_S,) * tiles_too:
+                todo(d)
+
         for d in (EAST, WEST):
             todo(d)
 
-        @pl.when(there_north)
-        def _():
-            for d in (NORTH, NE, NW):
-                todo(d)
-
-        @pl.when(there_south)
-        def _():
-            for d in (SOUTH, SE, SW):
-                todo(d)
-
     def copy(bufs, where_out, where_in, d, arriving=False):
-        o_rows, o_tiles, i_rows, i_tiles, ssem, rsem, shared = bufs
+        o_rows, o_tiles, i_rows, i_tiles, i_more, ssem, rsem = bufs
         slot = d if arriving else d ^ 1
+        send, recv = ssem.at[(d,) + where_out], rsem.at[(slot,) + where_in]
         if d in (NORTH, SOUTH):
             src, dst = o_rows.at[(d,) + where_out], i_rows.at[(slot,) + where_in]
+        elif d in (TILES_N, TILES_S):
+            src = o_tiles.at[(slice(None),) + where_out]
+            dst = i_more.at[(slot - 8, slice(None)) + where_out]
+            recv = rsem.at[(slot,) + where_in]
         else:
-            src = o_tiles.at[(d - 2 if shared is None else int(d not in RIGHT),) + where_out]
+            src = o_tiles.at[(int(d not in RIGHT),) + where_out]
             dst = i_tiles.at[(slot - 2,) + where_in]
         return pltpu.make_async_remote_copy(
             src_ref=src,
             dst_ref=dst,
-            send_sem=ssem.at[(d,) + where_out],
-            recv_sem=rsem.at[(slot,) + where_in],
+            send_sem=send,
+            recv_sem=recv,
             device_id=device(d),
             device_id_type=MESH,
         )
 
-    def start(bufs, where_out, where_in):
-        for_each(lambda d: copy(bufs, where_out, where_in, d).start())
-
-    def finish(bufs, where_out, where_in):
+    def start(bufs, where_out, where_in, tiles_too=False):
+        for_each(lambda d: copy(bufs, where_out, where_in, d).start(), tiles_too)
+
+    def finish(bufs, where_out, where_in, tiles_too=False):
         def todo(d):
             c = copy(bufs, where_out, where_in, d, arriving=True)
             c.wait_recv()
             c.wait_send()
 
-        for_each(todo)
-
-    main = (out_rows, out_tiles, in_rows, in_tiles, send_sem, recv_sem, True)
-    sets = (set_out_rows, set_out_tiles, set_in_rows, set_in_tiles, set_send, set_recv, True)
-    ini = (ini_out_rows, ini_out_tiles, ini_in_rows, ini_in_tiles, ini_send, ini_recv, None)
+        for_each(todo, tiles_too)
+
+    def finish_more(g):
+        def todo(d):
+            if d in (TILES_N, TILES_S):
+                c = copy(main, (g,), (0, g), d, arriving=True)
+                c.wait_recv()
+                c.wait_send()
+
+        for_each(todo, True)
+
+    main = (out_rows, out_tiles, in_rows, in_tiles, in_more, send_sem, recv_sem)
+    sets = (
+        set_out_rows, set_out_tiles, set_in_rows, set_in_tiles, None, set_send, set_recv
+    )
+    ini = (
+        ini_out_rows, ini_out_tiles, ini_in_rows, ini_in_tiles, ini_in_more,
+        ini_send, ini_recv,
+    )
 
     def join_x(a, b):
         return (
@@ -214,15 +237,15 @@
                 s[j][i] = s[j][i] + got[j]
         return join(s)
 
-    def from_inside(w):
+    def from_inside(w, k_ref):
         rx = [[None] * NP for _ in range(NP)]
         ry = [[None] * NP for _ in range(NP)]
         for j in range(NP):
-            k = [both_k_ref[j * 6 + n] for n in range(6)]
+            k = [k_ref[j * 6 + n] for n in range(6)]
             rx[j][0] = k[0] * w[j][1] + k[1] * w[j][2] + k[2] * w[j][3]
             rx[j][3] = k[2] * w[j][0] + k[4] * w[j][1] + k[5] * w[j][2]
         for i in range(NP):
-            k = [both_k_ref[24 + i * 6 + n] for n in range(6)]
+            k = [k_ref[24 + i * 6 + n] for n in range(6)]
             ry[0][i] = k[0] * w[1][i] + k[1] * w[2][i] + k[2] * w[3][i]
             ry[3][i] = k[2] * w[0][i] + k[4] * w[1][i] + k[5] * w[2][i]
         return joined_edges(rx, ry)
@@ -265,7 +288,22 @@
             put(NW, corner[2], n)
             put(SE, corner[3], from_right)
 
-    def emit(refs, where, c, tiles, fields):
+    def stacked(top, bottom):
+        kept = top[0]
+        for n in (1, 2):
+            kept = jnp.where(sub == last_row - n, pltpu.roll(top[n], rows - n, 0), kept)
+        for n in range(3):
+            kept = jnp.where(sub == 2 - n, pltpu.roll(bottom[n], 2 - n, 0), kept)
+        return kept
+
+    def along_x(v, i):
+        order = (2, 1, 0) if i == 3 else (1, 2, 3)
+        return stacked([v[3][n] for n in order], [v[0][n] for n in order])
+
+    def along_y(v, i):
+        return stacked([v[n][i] for n in (2, 1, 0)], [v[n][i] for n in (1, 2, 3)])
+
+    def emit(refs, where, c, tiles, fields, segments=False):
         for q, (vx, vy, corner) in enumerate(fields):
             for i in range(NP):
                 lay_rows(refs[0], where + (c,), q * NP + i, vy[3][i], vy[0][i])
@@ -282,7 +320,10 @@
                     jnp.where(sub == last_row - 2, pltpu.roll(top, rows - 2, 0), bottom),
                 ),
             )
-            for m, value in enumerate([f[0][j][i] for f in fields for j in range(3)] + [ends]):
+            columns = [f[0][j][i] for f in fields for j in range(3)] + [ends]
+            if segments:
+                columns += [along_x(v, i), along_y(v, i)]
+            for m, value in enumerate(columns):
                 n = m * per + c
                 shift = lax.rem(n + 1, cols) if i == 3 else n
                 tile = jnp.where(lane == n, pltpu.roll(value, shift, 1), tile)
@@ -296,14 +337,6 @@
         return jnp.broadcast_to(
             ref[where + (slice(k, k + 1), slice(None))], (rows, cols)
         )
-
-    def ini_tiles():
-        got = [ini_in_tiles[d - 2] for d in range(2, 8)]
-        for d in (NE, NW):
-            got[d - 2] = pltpu.roll(got[d - 2], rows - 1, 0)
-        for d in (SE, SW):
-            got[d - 2] = pltpu.roll(got[d - 2], 1, 0)
-        return got
 
     def in_sides(ref, where):
         sides = []
@@ -384,6 +417,8 @@
     in_tiles[...] = jnp.zeros_like(in_tiles)
     set_in_rows[...] = jnp.zeros_like(set_in_rows)
     set_in_tiles[...] = jnp.zeros_like(set_in_tiles)
+    in_more[...] = jnp.zeros_like(in_more)
+    ini_in_more[...] = jnp.zeros_like(ini_in_more)
     ini_in_rows[...] = jnp.zeros_like(ini_in_rows)
     ini_in_tiles[...] = jnp.zeros_like(ini_in_tiles)
     barrier = pltpu.get_barrier_semaphore()
@@ -435,34 +470,43 @@
         dy[0][i], dy[3][i] = first(ky[i]), final(ky[i])
     dx, dy = joined_edges(dx, dy)
     local = join(mass)
-    tiles = [zero] * 6
     for n in range(NP):
         lay_rows(ini_out_rows, (0,), n, local[3][n], local[0][n])
         lay_rows(ini_out_rows, (0,), 4 + n, dy[3][n], dy[0][n])
-        lay_lane(tiles, n, local[n][3], local[n][0], None)
-        lay_lane(tiles, 4 + n, dx[n][3], dx[n][0], None)
     for n in range(6):
         lay_rows(ini_out_rows, (1,), n, kx[3][n], kx[0][n])
-        lay_lane(tiles, 8 + n, ky[3][n], ky[0][n], None)
-    lay_lane(tiles, 0, None, None, corners_of(local))
-    both = [[None] * NP for _ in range(NP)]
-    for j in (0, 3):
-        for i in (0, 3):
-            both[j][i] = dx[j][i] + dy[j][i]
-    lay_lane(tiles, 1, None, None, corners_of(both))
     for n in (6, 7):
         lay_rows(ini_out_rows, (1,), n, zero, zero)
-    for d in range(2, 8):
-        ini_out_tiles[d - 2] = tiles[d - 2]
-    peers = 2 + 3 * there_north.astype(jnp.int32) + 3 * there_south.astype(jnp.int32)
-    pl.semaphore_wait(barrier, peers)
-    start(ini, (), ())
+    to_first, to_last = (0, 1, 2), (5, 4, 2)
+    for side, i in ((0, 3), (1, 0)):
+        to_corner = to_last if i == 3 else to_first
+        columns = (
+            [local[j][i] for j in range(NP)]
+            + [dx[j][i] for j in range(NP)]
+            + [ky[i][n] for n in range(6)]
+            + [jnp.where(at_north, dx[3][i] + dy[3][i], dx[0][i] + dy[0][i])]
+            + [
+                stacked([kx[3][n] for n in to_corner], [kx[0][n] for n in to_corner]),
+                along_x(local, i),
+                stacked([ky[i][n] for n in to_last], [ky[i][n] for n in to_first]),
+                along_y(local, i),
+            ]
+        )
+        tile = zero
+        for n, value in enumerate(columns):
+            shift = (n + 1) % cols if i == 3 else n
+            tile = jnp.where(lane == n, pltpu.roll(value, shift, 1), tile)
+        ini_out_tiles[side] = tile
+    for j in range(NP):
+        for i in range(NP):
+            inverse_ref[j * NP + i] = 1.0 / local[j][i]
 
     def enter_group(g):
         for c in fields(g):
             c.wait()
 
-        def enter(c, tiles):
+        def enter(c, carry):
+            tiles, first = carry
             ch = g * per + c
             state = face_frame(load(state_ref, ch), masks)
             forcing = face_frame(load(forcing_ref, ch), masks)
@@ -477,17 +521,78 @@
                 tiles,
                 ((base, base, corners_of(base)), (tend, tend, corners_of(tend))),
             )
-            store(part_ref, ch, stiff(state, own_k_ref))
-            return tiles
-
-        tiles = lax.fori_loop(0, per, enter, (zero,) * 2, unroll=UNROLL)
+            s = stiff(state, own_k_ref)
+            store(part_ref, ch, s)
+            rx, ry = from_inside(times(s, inverse_ref), own_k_ref)
+            for j in (0, 3):
+                at_row = at_north if j == 3 else at_south
+                for i in (0, 3):
+                    corner = at_row & (at_east if i == 3 else at_west)
+                    rx[j][i] = jnp.where(corner, 0.0, rx[j][i])
+                    ry[j][i] = jnp.where(corner, 0.0, ry[j][i])
+            first = emit(
+                main,
+                (g,),
+                c,
+                first,
+                ((s, s, None), (rx, ry, (zero,) * 4)),
+                segments=True,
+            )
+            return tiles, first
+
+        tiles, first = lax.fori_loop(
+            0, per, enter, ((zero,) * 2, (zero,) * 2), unroll=UNROLL
+        )
         keep_tiles(set_out_tiles, (g,), tiles)
+        keep_tiles(out_tiles, (g,), first)
+
+    def first_sends(g):
+        start(main, (g,), (0, g), True)
         start(sets, (g,), (g,))
 
-    pl.loop(0, GROUPS)(enter_group)
-
-    finish(ini, (), ())
-    got = ini_tiles()
+    @pl.loop(0, GROUPS)
+    def _(g):
+        enter_group(g)
+
+        @pl.when(g == 1)
+        def _():
+            peers = (
+                2 + 3 * there_north.astype(jnp.int32) + 3 * there_south.astype(jnp.int32)
+            )
+            pl.semaphore_wait(barrier, peers)
+            start(ini, (), (), True)
+            first_sends(0)
+
+        @pl.when(g >= 1)
+        def _():
+            first_sends(g)
+
+    finish(ini, (), (), True)
+    got = [ini_in_tiles[d - 2] for d in range(2, 8)]
+    beside = [[ini_in_more[v, side] for v in range(2)] for side in range(2)]
+    CORNER_D, SEG = 14, 15
+
+    def segment_weight(side, column):
+        flank, above, below = [
+            got[d - 2] for d in ((EAST, NE, SE) if side == 0 else (WEST, NW, SW))
+        ]
+        if column == SEG:
+            total = flank + jnp.where(
+                sub >= 5, pltpu.roll(above, 5, 0), pltpu.roll(below, 3, 0)
+            )
+        else:
+            up, down = beside[side]
+            total = jnp.where(
+                sub >= 5, pltpu.roll(above + up, 5, 0), pltpu.roll(below + down, 3, 0)
+            )
+        k = jnp.broadcast_to(total[:, column : column + 1], (rows, cols))
+        m = jnp.broadcast_to(total[:, column + 1 : column + 2], (rows, cols))
+        used = (m > 0.0) & ((sub >= 5) | (sub <= 2))
+        return jnp.where(used, k / jnp.where(used, m, 1.0), 0.0)
+
+    for side in range(2):
+        weight_ref[side, 0] = segment_weight(side, SEG)
+        weight_ref[side, 1] = segment_weight(side, SEG + 2)
 
     def lane_of(d, n):
         to = last_col if d in (EAST, NE, SE) else 0
@@ -505,7 +610,7 @@
     def west(n):
         return jnp.where(at_west, lane_of(WEST, n), 0.0)
 
-    def with_neighbours(v, first_k, corner_n):
+    def with_neighbours(v, first_k, corner_up, corner_down):
         v = [list(r) for r in v]
         for i in range(NP):
             v[3][i] = v[3][i] + north(0, first_k + i)
@@ -519,11 +624,16 @@
             (NW, 3, 0, at_north & at_west),
             (SE, 0, 3, at_south & at_east),
         ):
-            v[j][i] = v[j][i] + jnp.where(m, lane_of(d, corner_n), 0.0)
+            value = (
+                pltpu.roll(lane_of(d, corner_up), rows - 1, 0)
+                if j == 3
+                else pltpu.roll(lane_of(d, corner_down), 1, 0)
+            )
+            v[j][i] = v[j][i] + jnp.where(m, value, 0.0)
         return v
 
-    assembled = with_neighbours(local, 0, 0)
-    diagonal = with_neighbours([[zero] * NP for _ in range(NP)], 4, 1)
+    assembled = with_neighbours(local, 0, 0, 3)
+    diagonal = with_neighbours([[zero] * NP for _ in range(NP)], 4, CORNER_D, CORNER_D)
     for j in range(NP):
         for i in range(NP):
             inverse_ref[j * NP + i] = 1.0 / assembled[j][i]
@@ -539,21 +649,11 @@
             both_k_ref[24 + m * 6 + n] = y
 
     def emit_main(g, c, tiles, s):
-        rx, ry = from_inside(times(s, inverse_ref))
+        rx, ry = from_inside(times(s, inverse_ref), both_k_ref)
         corner = tuple(
             rx[j][i] + ry[j][i] for j, i in ((3, 3), (0, 0), (3, 0), (0, 3))
         )
         return emit(main, (g,), c, tiles, ((s, s, corners_of(s)), (rx, ry, corner)))
-
-    def send_group(g):
-        def send(c, tiles):
-            return emit_main(g, c, tiles, load(part_ref, g * per + c))
-
-        tiles = lax.fori_loop(0, per, send, (zero,) * 2, unroll=UNROLL)
-        keep_tiles(out_tiles, (g,), tiles)
-        start(main, (g,), (0, g))
-
-    pl.loop(0, GROUPS)(send_group)
 
     def settle_group(g):
         finish(sets, (g,), (g,))
@@ -568,7 +668,6 @@
 
         lax.fori_loop(0, per, settle, 0, unroll=UNROLL)
 
-    pl.loop(0, GROUPS)(settle_group)
 
     def advance(ch, c, g, parity, got, factor):
         where = (parity, g)
@@ -592,6 +691,27 @@
             for j in range(NP)
         ]
 
+    def corner_shares(g):
+        ends = (lane >= 6 * per) & (lane < 7 * per)
+        for side, (flank, above, below) in enumerate(((EAST, NE, SE), (WEST, NW, SW))):
+            here, up, down = [in_tiles[d - 2, 0, g] for d in (flank, above, below)]
+            x = weight_ref[side, 0] * (
+                here + jnp.where(sub >= 5, pltpu.roll(up, 5, 0), pltpu.roll(down, 3, 0))
+            )
+            y = weight_ref[side, 1] * jnp.where(
+                sub >= 5,
+                pltpu.roll(up + in_more[0, side, g], 5, 0),
+                pltpu.roll(down + in_more[1, side, g], 3, 0),
+            )
+            share = pltpu.roll(x, cols - per, 1) + pltpu.roll(y, cols - 2 * per, 1)
+            share = share + pltpu.roll(share, 1, 0) + pltpu.roll(share, 2, 0)
+            in_tiles[flank - 2, 0, g] = jnp.where(
+                ends & (sub == last_row - 1), pltpu.roll(share, rows - 1, 0), here
+            )
+            in_tiles[below - 2, 0, g] = jnp.where(
+                ends & (sub == last_row - 2), pltpu.roll(share, 3, 0), down
+            )
+
     def section_group(step):
         section, g = step // GROUPS, lax.rem(step, GROUPS)
         parity = lax.rem(section, 2)
@@ -601,7 +721,19 @@
                 section == m, jnp.float32(time_step / (SECTIONS - m)), factor
             )
         finish(main, (g,), (parity, g))
+
+        @pl.when(section == 0)
+        def _():
+            finish_more(g)
+            corner_shares(g)
+            settle_group(g)
+
         got = in_sides(in_tiles, (parity, g))
+
+        @pl.when(section == 0)
+        def _():
+            in_tiles[SE - 2, 0, g] = zero
+            in_tiles[SW - 2, 0, g] = zero
 
         def body(c, tiles):
             ch = g * per + c
@@ -640,16 +772,18 @@
     field = pltpu.VMEM((NP, NP, chan, rows, cols), f32)
     vmem = pl.BlockSpec(memory_space=pltpu.VMEM)
 
-    def buffers(out_lead, in_lead, tiles_per_rows, out_tiles):
+    def buffers(out_lead, in_lead, tiles_per_rows, more):
         dma = pltpu.SemaphoreType.DMA
-        return [
-            pltpu.VMEM((2,) + out_lead + (tiles_per_rows, rows, cols), f32),
-            pltpu.VMEM((out_tiles,) + out_lead + (rows, cols), f32),
-            pltpu.VMEM((2,) + in_lead + (tiles_per_rows, rows, cols), f32),
-            pltpu.VMEM((6,) + in_lead + (rows, cols), f32),
-            dma((8,) + out_lead),
-            dma((8,) + in_lead),
+        tile = (rows, cols)
+        got = [
+            pltpu.VMEM((2,) + out_lead + (tiles_per_rows,) + tile, f32),
+            pltpu.VMEM((2,) + out_lead + tile, f32),
+            pltpu.VMEM((2,) + in_lead + (tiles_per_rows,) + tile, f32),
+            pltpu.VMEM((6,) + in_lead + tile, f32),
         ]
+        if more:
+            got.append(pltpu.VMEM((2, 2) + out_lead + tile, f32))
+        return got + [dma((10,) + out_lead), dma((10,) + in_lead)]
 
     return pl.pallas_call(
         functools.partial(kernel, (chan, rows, cols) + counts),
@@ -673,10 +807,11 @@
             pltpu.VMEM((48, rows, cols), f32),
             pltpu.VMEM((16, rows, cols), f32),
             pltpu.VMEM((16, rows, cols), f32),
+            pltpu.VMEM((2, 2, rows, cols), f32),
         ]
-        + buffers((GROUPS,), (2, GROUPS), per, 2)
-        + buffers((GROUPS,), (GROUPS,), per, 2)
-        + buffers((), (), 2, 6),
+        + buffers((GROUPS,), (2, GROUPS), per, True)
+        + buffers((GROUPS,), (GROUPS,), per, False)
+        + buffers((), (), 2, True),
         compiler_params=pltpu.CompilerParams(
             collective_id=0, has_side_effects=True, vmem_limit_bytes=56 * 2**20
         ),

time: 52 us -> 49.9 us (0.960)
  Pallas kernels: 48.7 us -> 46.6 us
    pallas_call x1, Pallas kernels: 48.7 us -> 46.6 us  [on_device(): pl.pallas_call(functools.partial(kernel, (chan, rows, cols) + counts), ou...]
where the time goes in v1:
time: 49.9 us; the launch traced here: 49.8 us
  Pallas kernels  46.6 us (93%)
  local copies, waits for them, and re-layouts  3.11 us (6%)
    pallas_call x1, Pallas kernels, on_device(): pl.pallas_call(functools.partial(kernel, (chan, rows, cols) + counts), ou...  46.6 us
    unnamed x1, local copies, waits for them, and re-layouts  3.11 us

profile of v1, /device:TPU:25, one launch (start us, length us, event | category | flops | bytes accessed | tf_op | source)
XLA Modules:
  0.0 49.8 jit_solution(3906663470289457105)
XLA Ops:
  0.0 46.6 %shard_map.64 = f32[4,4,32,8,128]{4,3,2,1,0:T(8,128)} custom-call(f32[4,4,32,8,128]{4,3,2,1,0:T(8,128)} %state_hbm.1, f32[4,4,32,8,128]{4,3,2,1,0:T(8,128)} %forcing_hbm.1, f32[4,4,8,128]{3,2,1,0:T(8,128)} %jacobian_hbm.1, f32[4,4,8,128]{3,2,1,0:T(8,128)} %metric_hbm.1, s32[8,128]{1,0:T(8,128)} %turns_hbm.1, f32[32]{0:T(128)} %viscosity_hbm.1), custom_call_target="tpu_custom_call" | custom-call | tf_op jit(solution)/shard_map/pallas_call | solution.py:788
  46.7 3.1 %copy.8 = f32[4,4,32,8,128]{4,3,2,1,0:T(8,128)} copy(f32[4,4,32,8,128]{4,3,2,1,0:T(8,128)} %shard_map.64) | data formatting | bytes 4194304

commit v2 on v1

--- a/solution.py
+++ b/solution.py
@@ -89,6 +89,7 @@
     diagonal_ref,
     mass_ref,
     weight_ref,
+    inner_ref,
     out_rows,
     out_tiles,
     in_rows,
@@ -237,18 +238,25 @@
                 s[j][i] = s[j][i] + got[j]
         return join(s)
 
-    def from_inside(w, k_ref):
-        rx = [[None] * NP for _ in range(NP)]
-        ry = [[None] * NP for _ in range(NP)]
-        for j in range(NP):
-            k = [k_ref[j * 6 + n] for n in range(6)]
-            rx[j][0] = k[0] * w[j][1] + k[1] * w[j][2] + k[2] * w[j][3]
-            rx[j][3] = k[2] * w[j][0] + k[4] * w[j][1] + k[5] * w[j][2]
-        for i in range(NP):
-            k = [k_ref[24 + i * 6 + n] for n in range(6)]
-            ry[0][i] = k[0] * w[1][i] + k[1] * w[2][i] + k[2] * w[3][i]
-            ry[3][i] = k[2] * w[0][i] + k[4] * w[1][i] + k[5] * w[2][i]
-        return joined_edges(rx, ry)
+    def inner_coefficients(kx, ky):
+        fields = []
+        for lines, far in ((kx, at_east), (ky, at_north)):
+            for k in lines:
+                to_first = (zero, k[0], k[1], k[2])
+                to_last = (k[2], k[4], k[5], zero)
+                fields += [jnp.where(far, b, a) for a, b in zip(to_first, to_last)]
+        return fields
+
+    def from_inside(w):
+        def total(m, v):
+            k = [inner_ref[m * NP + n] for n in range(NP)]
+            return k[0] * v[0] + k[1] * v[1] + k[2] * v[2] + k[3] * v[3]
+
+        x = [total(j, w[j]) for j in range(NP)]
+        y = [total(NP + i, [w[j][i] for j in range(NP)]) for i in range(NP)]
+        x[0], x[3] = join_y(x[0], x[3])
+        y[0], y[3] = join_x(y[0], y[3])
+        return [[v] * NP for v in x], [list(y) for _ in range(NP)]
 
     def joined_edges(rx, ry):
         for i in (0, 3):
@@ -500,6 +508,8 @@
     for j in range(NP):
         for i in range(NP):
             inverse_ref[j * NP + i] = 1.0 / local[j][i]
+    for n, value in enumerate(inner_coefficients(kx, ky)):
+        inner_ref[n] = value
 
     def enter_group(g):
         for c in fields(g):
@@ -523,7 +533,7 @@
             )
             s = stiff(state, own_k_ref)
             store(part_ref, ch, s)
-            rx, ry = from_inside(times(s, inverse_ref), own_k_ref)
+            rx, ry = from_inside(times(s, inverse_ref))
             for j in (0, 3):
                 at_row = at_north if j == 3 else at_south
                 for i in (0, 3):
@@ -638,18 +648,21 @@
         for i in range(NP):
             inverse_ref[j * NP + i] = 1.0 / assembled[j][i]
             diagonal_ref[j * NP + i] = diagonal[j][i]
+    both_x, both_y = [list(k) for k in kx], [list(k) for k in ky]
+    for n in range(6):
+        both_x[0][n] = both_x[0][n] + south(1, n)
+        both_x[3][n] = both_x[3][n] + north(1, n)
+        both_y[0][n] = both_y[0][n] + west(8 + n)
+        both_y[3][n] = both_y[3][n] + east(8 + n)
     for m in range(NP):
         for n in range(6):
-            x, y = kx[m][n], ky[m][n]
-            if m == 0:
-                x, y = x + south(1, n), y + west(8 + n)
-            if m == 3:
-                x, y = x + north(1, n), y + east(8 + n)
-            both_k_ref[m * 6 + n] = x
-            both_k_ref[24 + m * 6 + n] = y
+            both_k_ref[m * 6 + n] = both_x[m][n]
+            both_k_ref[24 + m * 6 + n] = both_y[m][n]
+    for n, value in enumerate(inner_coefficients(both_x, both_y)):
+        inner_ref[n] = value
 
     def emit_main(g, c, tiles, s):
-        rx, ry = from_inside(times(s, inverse_ref), both_k_ref)
+        rx, ry = from_inside(times(s, inverse_ref))
         corner = tuple(
             rx[j][i] + ry[j][i] for j, i in ((3, 3), (0, 0), (3, 0), (0, 3))
         )
@@ -808,6 +821,7 @@
             pltpu.VMEM((16, rows, cols), f32),
             pltpu.VMEM((16, rows, cols), f32),
             pltpu.VMEM((2, 2, rows, cols), f32),
+            pltpu.VMEM((32, rows, cols), f32),
         ]
         + buffers((GROUPS,), (2, GROUPS), per, True)
         + buffers((GROUPS,), (GROUPS,), per, False)

time: 49.9 us -> 49.7 us (level)
  no operation moved by 1% of the time
where the time goes in v2:
time: 49.7 us; the launch traced here: 49.6 us
  Pallas kernels  46.4 us (93%)
  local copies, waits for them, and re-layouts  3.11 us (6%)
    pallas_call x1, Pallas kernels, on_device(): pl.pallas_call(functools.partial(kernel, (chan, rows, cols) + counts), ou...  46.4 us
    unnamed x1, local copies, waits for them, and re-layouts  3.11 us

profile of v2, /device:TPU:25, one launch (start us, length us, event | category | flops | bytes accessed | tf_op | source)
XLA Modules:
  0.0 49.6 jit_solution(11198170508500927797)
XLA Ops:
  0.0 46.4 %shard_map.64 = f32[4,4,32,8,128]{4,3,2,1,0:T(8,128)} custom-call(f32[4,4,32,8,128]{4,3,2,1,0:T(8,128)} %state_hbm.1, f32[4,4,32,8,128]{4,3,2,1,0:T(8,128)} %forcing_hbm.1, f32[4,4,8,128]{3,2,1,0:T(8,128)} %jacobian_hbm.1, f32[4,4,8,128]{3,2,1,0:T(8,128)} %metric_hbm.1, s32[8,128]{1,0:T(8,128)} %turns_hbm.1, f32[32]{0:T(128)} %viscosity_hbm.1), custom_call_target="tpu_custom_call" | custom-call | tf_op jit(solution)/shard_map/pallas_call | solution.py:801
  46.4 3.1 %copy.8 = f32[4,4,32,8,128]{4,3,2,1,0:T(8,128)} copy(f32[4,4,32,8,128]{4,3,2,1,0:T(8,128)} %shard_map.64) | data formatting | bytes 4194304
